TPU v7x, 128 devices: a whole 4x4x4 slice. The times are simulated.
128 devices in a mesh: seq: 8 (over x, core), head: 16 (over z, y).
Axes of the slice: x: 4, y: 4, z: 4, core: 2. Of those that a mesh axis runs over, the one named last changes fastest.
Arguments:
- tokens: bfloat16 [1024, 6144], P('seq'), may hold values from -6 to 6
- log_decay: float32 [1024, 32], P('seq', 'head'), may hold values from -1 to 0
- carried_state: float32 [32, 128, 128], P('head'), may hold values from -48 to 48
- q_weight: bfloat16 [6144, 4096], P(None, 'head'), may hold values from -0.078125 to 0.078125
- k_weight: bfloat16 [6144, 4096], P(None, 'head'), may hold values from -0.078125 to 0.078125
- v_weight: bfloat16 [6144, 4096], P(None, 'head'), may hold values from -0.078125 to 0.078125
- out_weight: bfloat16 [4096, 6144], P('head'), may hold values from -0.09375 to 0.09375
- final_gain: bfloat16 [6144], replicated, may hold values from 0.099609375 to 1.8984375
- vocab_weight: bfloat16 [6144, 131072], P(None, ('seq', 'head')), may hold values from -5 to 5
- targets: int32 [1024], replicated, may hold values from 0 to 131071
Outputs:
- loglik: float32 [1024], P('seq')
All inputs are finite; a program needn't handle non-finite values.
Results may differ from a plain program's by a relative error of at most 0.002.
Values may be sent and summed in bfloat16 or wider, within the bound.
No kernel may reach another device: no remote copies, remote signals or barrier semaphores. Data moves between devices by JAX's collectives and lax.ppermute only.
A program may use at most 128 MiB of HBM per device.

v0:
```python
import jax
import jax.numpy as jnp
from jax import lax
from jax.sharding import PartitionSpec as P


def prefix(array, axis, combine, identity):
    length, here = (lax.axis_size(axis), lax.axis_index(axis))
    everything = jax.tree.map(lambda part: lax.all_gather(part, axis), array)
    start = jax.tree.map(
        lambda part, zero: jnp.broadcast_to(jnp.asarray(zero, part.dtype), part.shape),
        array,
        identity,
    )

    def turn(k, before):
        reached = k < here
        new = combine(before, jax.tree.map(lambda part: part[k], everything))
        return jax.tree.map(lambda a, b: jnp.where(reached, a, b), new, before)

    return lax.fori_loop(0, length, turn, start)


def combine_states(earlier, later):
    return (earlier[0] * later[0], later[0][:, None, None] * earlier[1] + later[1])


def shards(
    tokens,
    log_decay,
    carried_state,
    q_weight,
    k_weight,
    v_weight,
    out_weight,
    final_gain,
    vocab_weight,
    targets,
):
    highest = lax.Precision.HIGHEST
    rows_here = tokens.shape[0]
    heads_here = carried_state.shape[0]
    head_size = carried_state.shape[1]
    view = (rows_here, heads_here, head_size)
    queries = (
        jnp.dot(tokens, q_weight, preferred_element_type=jnp.float32)
        .astype(jnp.bfloat16)
        .reshape(view)
    )
    keys_loc = (
        jnp.dot(tokens, k_weight, preferred_element_type=jnp.float32)
        .astype(jnp.bfloat16)
        .reshape(view)
    )
    values = (
        jnp.dot(tokens, v_weight, preferred_element_type=jnp.float32)
        .astype(jnp.bfloat16)
        .reshape(view)
    )
    cumul = jnp.cumsum(log_decay, axis=0)
    last_cum = cumul[-1]
    ends = jnp.exp(last_cum[None, :] - cumul)
    local_state = jnp.einsum(
        "thd,the->hde",
        keys_loc.astype(jnp.float32) * ends[:, :, None],
        values.astype(jnp.float32),
        precision=highest,
    )
    total_decay = jnp.exp(last_cum)
    prefix_decay, prefix_state = prefix(
        (total_decay, local_state),
        "seq",
        combine_states,
        (jnp.ones_like(total_decay), jnp.zeros_like(local_state)),
    )
    lower = jnp.arange(rows_here)[:, None] >= jnp.arange(rows_here)[None, :]
    scores = jnp.einsum("thd,shd->hts", queries, keys_loc, preferred_element_type=jnp.float32)
    diff = jnp.transpose(cumul[:, None, :] - cumul[None, :, :], (2, 0, 1))
    weight = (scores * jnp.exp(jnp.where(lower[None], diff, -1e30))).astype(jnp.bfloat16)
    intra = jnp.einsum("hts,shd->thd", weight, values, preferred_element_type=jnp.float32)
    state_in = prefix_decay[:, None, None] * carried_state + prefix_state
    inter = jnp.exp(cumul)[:, :, None] * jnp.einsum(
        "thd,hde->the", queries.astype(jnp.float32), state_in, precision=highest
    )
    attended = intra + inter
    normed_heads = attended * lax.rsqrt(
        jnp.mean(attended * attended, axis=-1, keepdims=True) + 1e-06
    )
    flat_heads = normed_heads.astype(jnp.bfloat16).reshape(rows_here, heads_here * head_size)
    rows_mine = rows_here // lax.axis_size("head")
    head_index = lax.axis_index("head")
    mixed_all = lax.psum(
        jnp.dot(flat_heads, out_weight, preferred_element_type=jnp.float32), "head"
    )
    mixed = lax.dynamic_slice_in_dim(mixed_all, head_index * rows_mine, rows_mine, 0)
    resid = (
        lax.dynamic_slice_in_dim(tokens, head_index * rows_mine, rows_mine, 0).astype(jnp.float32)
        + mixed
    )
    final_rows = (
        resid
        * lax.rsqrt(jnp.mean(resid * resid, axis=-1, keepdims=True) + 1e-06)
        * final_gain.astype(jnp.float32)
    )
    final_rows = final_rows.astype(jnp.bfloat16)
    vocab_local = vocab_weight.shape[1]
    offset = (lax.axis_index("seq") * lax.axis_size("head") + head_index) * vocab_local
    columns = jnp.arange(vocab_local, dtype=jnp.int32)
    logits = jnp.dot(
        lax.all_gather(final_rows, ("seq", "head"), axis=0, tiled=True),
        vocab_weight,
        preferred_element_type=jnp.float32,
    )
    top = jnp.max(logits, axis=1)
    total = jnp.sum(jnp.exp(logits - top[:, None]), axis=1)
    wanted = targets - offset
    hit = jnp.sum(jnp.where(columns[None, :] == wanted[:, None], logits, 0.0), axis=1)
    top_all = lax.pmax(top, ("seq", "head"))
    total_all, hit_all = lax.psum((total * jnp.exp(top - top_all), hit), ("seq", "head"))
    loglik = hit_all - top_all - jnp.log(total_all)
    return lax.dynamic_slice_in_dim(loglik, lax.axis_index("seq") * rows_here, rows_here, 0)


def solution(mesh):
    return jax.shard_map(
        shards,
        mesh=mesh,
        in_specs=(
            P("seq", None),
            P("seq", "head"),
            P("head", None, None),
            P(None, "head"),
            P(None, "head"),
            P(None, "head"),
            P("head", None),
            P(),
            P(None, ("seq", "head")),
            P(),
        ),
        out_specs=P("seq"),
        check_vma=False,
    )
```

profile of v0, /device:TPU:1, one launch (start us, length us, event | category | flops | bytes accessed | tf_op | source)
XLA Modules:
  0.0 385.3 jit_solution(14718534888018662489)
XLA Ops:
  7.7 3.0 convolution_convert_fusion
  10.8 3.0 fusion.4
  14.7 11.8 %all-gather.1 = f32[8,1,2]{2,1,0:T(1,128)S(1)} all-gather(f32[1,1,2]{2,1,0:T(1,128)S(1)} %get-tuple-element.171), channel_id=1, replica_groups=mesh['seq'=8,'head'=16] {'seq'}, dimensions={0}, use_global_device_ids=true | all-gather | bytes 72 | tf_op jit(solution)/shard_map/all_gather | solution.py:9
  26.7 3.1 fusion.5
  29.8 12.0 %all-gather.7.cloned.1.call-done = f32[16,128,128]{2,1,0:T(8,128)} async-done(((f32[2,128,128]{2,1,0:T(8,128)}), f32[16,128,128]{2,1,0:T(8,128)}) %all-gather.7.cloned.1.call-update) | async-done | bytes 1048592 | tf_op jit(solution)/shard_map/all_gather | solution.py:9
  41.8 8.3 %while.16 = (s32[]{:T(128)}, f32[2]{0:T(128)S(1)}, f32[2,128,128]{2,1,0:T(8,128)S(1)}, s32[]{:T(128)}, f32[8,2]{1,0:T(8,128)S(1)}, /*index=5*/f32[8,2,128,128]{3,2,1,0:T(8,128)}, s32[]{:T(128)}, s32[]{:T(128)}) while((s32[]{:T(128)}, f32[2]{0:T(128)S(1)}, f32[2,128,128]{2,1,0:T(8,128)S(1)}, s32[]{:T(128)}, f32[8,2]{1,0:T(8,128)S(1)}, ...), condition=%wide.region_2.3_spmd.clone, body=%wide.region_1.2_spmd.clone.sunk | while | flops 131082 | bytes 393371 | solution.py:21
  42.8 1.0 fusion.48
  43.9 1.0 fusion.48
  44.9 1.0 fusion.48
  46.0 1.0 fusion.48
  47.0 1.0 fusion.48
  48.0 1.0 fusion.48
  49.1 1.0 fusion.48
  50.1 1.9 fusion.1
  52.0 1.2 multiply_reduce_fusion.1
  53.3 2.3 fusion.35
  56.3 94.3 %all-reduce.3.cloned.1.call-done = f32[128,6144]{1,0:T(8,128)} async-done(((f32[128,6144]{1,0:T(8,128)}), f32[128,6144]{1,0:T(8,128)}) %all-reduce.3.cloned.1.call-update) | async-done | bytes 3145744 | tf_op jit(solution)/shard_map/psum | solution.py:92
  150.6 1.2 multiply_reduce_fusion
  151.8 1.7 multiply_convert_fusion
  153.6 73.3 %all-gather.5.cloned.1.call-done = bf16[1024,6144]{1,0:T(8,128)(2,1)} async-done(((bf16[8,6144]{1,0:T(8,128)(2,1)}), bf16[1024,6144]{1,0:T(8,128)(2,1)}) %all-gather.5.cloned.1.call-update) | async-done | bytes 12582928 | tf_op jit(solution)/shard_map/all_gather | solution.py:110
  226.9 19.4 %fusion.34 = (f32[1024]{0:T(1024)S(1)}, f32[1024,1024]{0,1:T(8,128)}) fusion(bf16[1024,6144]{1,0:T(8,128)(2,1)} %all-gather.5.cloned.1.call-done, bf16[6144,1024]{1,0:T(8,128)(2,1)} %param.20), kind=kOutput, calls=%fused_computation.57 | convolution fusion | flops 12885949440 | bytes 29364224 | tf_op jit(solution)/shard_map/dot_general | solution.py:109
  246.3 64.4 %pmax.7 = f32[1024]{0:T(1024)S(1)} all-reduce(f32[1024]{0:T(1024)S(1)} %get-tuple-element.174), channel_id=1, replica_groups=mesh['seq'=8,'head'=16] {'seq','head'}, use_global_device_ids=true, to_apply=%region_9.10 | all-reduce | flops 1024 | bytes 8192 | tf_op jit(solution)/shard_map/pmax | solution.py:118
  310.7 3.3 select_reduce_fusion
  314.0 64.2 %all-reduce = (f32[1024]{0:T(1024)S(1)}, f32[1024]{0:T(1024)S(1)}) all-reduce(f32[1024]{0:T(1024)S(1)} %exponential_multiply_fusion, f32[1024]{0:T(1024)S(1)} %get-tuple-element.150), channel_id=1, replica_groups=mesh['seq'=8,'head'=16] {'seq','head'}, use_global_device_ids=true, to_apply=%region_11.12 | all-reduce | flops 2048 | bytes 16384 | tf_op jit(solution)/shard_map/psum | solution.py:119
  (41 shorter events, 4.9 us)
Async XLA Ops:
  6.5 46.7 %copy-start = (bf16[256,6144]{1,0:T(8,128)(2,1)S(1)}, bf16[256,6144]{1,0:T(8,128)(2,1)}, u32[]{:S(2)}) copy-start(bf16[256,6144]{1,0:T(8,128)(2,1)} %param.18) | copy-start | bytes 9437188
  6.5 35.2 %all-gather.7.cloned.1.call-start = ((), (), s32[]{:S(2)}) async-start(), calls=%async_computation.2 | async-start | bytes 1179648 | tf_op jit(solution)/shard_map/all_gather | solution.py:9
  14.7 135.9 %all-reduce.3.cloned.1.call-start = ((), (), s32[]{:S(2)}) async-start(), calls=%async_computation | async-start | bytes 6291456 | tf_op jit(solution)/shard_map/psum | solution.py:92
  55.6 0.7 copy-start.1
  55.6 98.0 %copy-start.2 = (s32[1024]{0:T(1024)S(1)}, s32[1024]{0:T(1024)}, u32[]{:S(2)}) copy-start(s32[1024]{0:T(1024)} %param.21) | copy-start | bytes 12292
  55.6 171.3 %all-gather.5.cloned.1.call-start = ((), (), s32[]{:S(2)}) async-start(), calls=%async_computation.1 | async-start | bytes 12681216 | tf_op jit(solution)/shard_map/all_gather | solution.py:110
Sparse Core Ops, SparseCore 0:
  14.8 26.9 all-gather.6
  55.7 94.8 all-reduce.2
  153.7 73.0 all-gather.4
where the time goes:
time: 386 us; the launch traced here: 385 us
  waiting for transfers between devices  180 us (47%)
  blocking collectives  140 us (36%)
  matrix products  34.7 us (9%)
  other arithmetic  14.5 us (4%)
  between operations  13.2 us (3%)
    psum x1, waiting for transfers between devices, shards(): lax.psum(jnp.dot(flat_heads, out_weight, preferred_element_type=jnp.float...  94.3 us
    all_gather x1, waiting for transfers between devices, shards(): lax.all_gather(final_rows, ('seq', 'head'), axis=0, tiled=True)  73.3 us
    pmax x1, blocking collectives, shards(): top_all = lax.pmax(top, ('seq', 'head'))  64.4 us
    psum x1, blocking collectives, shards(): lax.psum((total * jnp.exp(top - top_all), hit), ('seq', 'head'))  64.2 us
    dot_general x1, matrix products, shards(): jnp.dot(lax.all_gather(final_rows, ('seq', 'head'), axis=0, tiled=True),...  19.4 us
    all_gather x1, waiting for transfers between devices, prefix(): everything = jax.tree.map(lambda part: lax.all_gather(part, axis), array)  12 us
    all_gather x1, blocking collectives, prefix(): everything = jax.tree.map(lambda part: lax.all_gather(part, axis), array)  11.8 us
    select_n x16, other arithmetic, turn(): return jax.tree.map(lambda a, b: jnp.where(reached, a, b), new, before)  8.09 us
  transfers between devices with their start and end apart: 3, of which 3 were waited for; matrix products, arithmetic and copies ran while one was open for 1% of the time, Pallas kernels for 0%

commit v1 on v0

--- a/solution.py
+++ b/solution.py
@@ -89,8 +89,9 @@
     flat_heads = normed_heads.astype(jnp.bfloat16).reshape(rows_here, heads_here * head_size)
     rows_mine = rows_here // lax.axis_size("head")
     head_index = lax.axis_index("head")
-    mixed_all = lax.psum(
-        jnp.dot(flat_heads, out_weight, preferred_element_type=jnp.float32), "head"
+    mixed_all = jnp.sum(
+        lax.all_gather(jnp.dot(flat_heads, out_weight, preferred_element_type=jnp.float32), "head"),
+        axis=0,
     )
     mixed = lax.dynamic_slice_in_dim(mixed_all, head_index * rows_mine, rows_mine, 0)
     resid = (

time: 386 us -> 591 us (1.53)
  waiting for transfers between devices: 180 us -> 367 us
  other arithmetic: 14.5 us -> 31.6 us
    all_gather x0 -> x1, waiting for transfers between devices: none -> 282 us  [shards(): lax.all_gather(jnp.dot(flat_heads, out_weight, preferred_element_type=jnp...]
    psum x1 -> x0, waiting for transfers between devices: 94.3 us -> none  [shards(): lax.psum(jnp.dot(flat_heads, out_weight, preferred_element_type=jnp.float...]
    reduce_sum x0 -> x1, other arithmetic: none -> 17.3 us  [shards(): jnp.sum(lax.all_gather(jnp.dot(flat_heads, out_weight, preferred_element_...]
where the time goes in v1:
time: 591 us; the launch traced here: 590 us
  waiting for transfers between devices  367 us (62%)
  blocking collectives  140 us (24%)
  matrix products  34.7 us (6%)
  other arithmetic  31.6 us (5%)
  between operations  13.2 us (2%)
    all_gather x1, waiting for transfers between devices, shards(): lax.all_gather(jnp.dot(flat_heads, out_weight, preferred_element_type=jnp...  282 us
    all_gather x1, waiting for transfers between devices, shards(): lax.all_gather(final_rows, ('seq', 'head'), axis=0, tiled=True)  73.5 us
    pmax x1, blocking collectives, shards(): top_all = lax.pmax(top, ('seq', 'head'))  64.4 us
    psum x1, blocking collectives, shards(): lax.psum((total * jnp.exp(top - top_all), hit), ('seq', 'head'))  64.2 us
    dot_general x1, matrix products, shards(): jnp.dot(lax.all_gather(final_rows, ('seq', 'head'), axis=0, tiled=True),...  19.5 us
    reduce_sum x1, other arithmetic, shards(): jnp.sum(lax.all_gather(jnp.dot(flat_heads, out_weight, preferred_element_...  17.3 us
    all_gather x1, waiting for transfers between devices, prefix(): everything = jax.tree.map(lambda part: lax.all_gather(part, axis), array)  12 us
    all_gather x1, blocking collectives, prefix(): everything = jax.tree.map(lambda part: lax.all_gather(part, axis), array)  11.8 us
  transfers between devices with their start and end apart: 3, of which 3 were waited for; matrix products, arithmetic and copies ran while one was open for 1% of the time, Pallas kernels for 0%

profile of v1, /device:TPU:1, one launch (start us, length us, event | category | flops | bytes accessed | tf_op | source)
XLA Modules:
  0.0 590.2 jit_solution(7105345002370355773)
XLA Ops:
  7.7 3.0 convolution_convert_fusion
  10.8 3.0 fusion.4
  14.7 11.8 %all-gather.2 = f32[8,1,2]{2,1,0:T(1,128)S(1)} all-gather(f32[1,1,2]{2,1,0:T(1,128)S(1)} %get-tuple-element.171), channel_id=1, replica_groups=mesh['seq'=8,'head'=16] {'seq'}, dimensions={0}, use_global_device_ids=true | all-gather | bytes 72 | tf_op jit(solution)/shard_map/all_gather | solution.py:9
  26.7 3.1 fusion.5
  29.8 12.0 %all-gather.9.cloned.1.call-done = f32[16,128,128]{2,1,0:T(8,128)} async-done(((f32[2,128,128]{2,1,0:T(8,128)}), f32[16,128,128]{2,1,0:T(8,128)}) %all-gather.9.cloned.1.call-update) | async-done | bytes 1048592 | tf_op jit(solution)/shard_map/all_gather | solution.py:9
  41.8 8.3 %while.16 = (s32[]{:T(128)}, f32[2]{0:T(128)S(1)}, f32[2,128,128]{2,1,0:T(8,128)S(1)}, s32[]{:T(128)}, f32[8,2]{1,0:T(8,128)S(1)}, /*index=5*/f32[8,2,128,128]{3,2,1,0:T(8,128)}, s32[]{:T(128)}, s32[]{:T(128)}) while((s32[]{:T(128)}, f32[2]{0:T(128)S(1)}, f32[2,128,128]{2,1,0:T(8,128)S(1)}, s32[]{:T(128)}, f32[8,2]{1,0:T(8,128)S(1)}, ...), condition=%wide.region_2.3_spmd.clone, body=%wide.region_1.2_spmd.clone.sunk | while | flops 131082 | bytes 393371 | solution.py:21
  42.8 1.0 fusion.48
  43.9 1.0 fusion.48
  44.9 1.0 fusion.48
  46.0 1.0 fusion.48
  47.0 1.0 fusion.48
  48.0 1.0 fusion.48
  50.1 1.9 fusion.1
  52.0 1.2 multiply_reduce_fusion.1
  53.3 2.2 fusion.35
  56.2 281.9 %all-gather.11.cloned.1.call-done = f32[2048,6144]{1,0:T(8,128)} async-done(((f32[128,6144]{1,0:T(8,128)}), f32[2048,6144]{1,0:T(8,128)}) %all-gather.11.cloned.1.call-update) | async-done | bytes 50331664 | tf_op jit(solution)/shard_map/all_gather | solution.py:93
  338.1 17.3 %reduce_sum.46 = f32[128,6144]{1,0:T(8,128)S(1)} reduce(f32[16,128,6144]{2,1,0:T(8,128)} %bitcast.57, f32[]{:T(128)} %constant.55.clone.1), dimensions={0}, to_apply=%region_4.5 | reduce | flops 11796480 | bytes 53477380 | tf_op jit(solution)/shard_map/reduce_sum | solution.py:92
  355.4 1.1 multiply_reduce_fusion
  356.5 1.6 multiply_convert_fusion
  358.1 73.5 %all-gather.7.cloned.1.call-done = bf16[1024,6144]{1,0:T(8,128)(2,1)} async-done(((bf16[8,6144]{1,0:T(8,128)(2,1)}), bf16[1024,6144]{1,0:T(8,128)(2,1)}) %all-gather.7.cloned.1.call-update) | async-done | bytes 12582928 | tf_op jit(solution)/shard_map/all_gather | solution.py:111
  431.6 19.5 %fusion.34 = (f32[1024]{0:T(1024)S(1)}, f32[1024,1024]{0,1:T(8,128)}) fusion(bf16[1024,6144]{1,0:T(8,128)(2,1)} %all-gather.7.cloned.1.call-done, bf16[6144,1024]{1,0:T(8,128)(2,1)} %param.20), kind=kOutput, calls=%fused_computation.57 | convolution fusion | flops 12885949440 | bytes 29364224 | tf_op jit(solution)/shard_map/dot_general | solution.py:110
  451.1 64.4 %pmax.7 = f32[1024]{0:T(1024)S(1)} all-reduce(f32[1024]{0:T(1024)S(1)} %get-tuple-element.174), channel_id=1, replica_groups=mesh['seq'=8,'head'=16] {'seq','head'}, use_global_device_ids=true, to_apply=%region_9.10 | all-reduce | flops 1024 | bytes 8192 | tf_op jit(solution)/shard_map/pmax | solution.py:119
  515.5 3.3 select_reduce_fusion
  518.9 64.2 %all-reduce = (f32[1024]{0:T(1024)S(1)}, f32[1024]{0:T(1024)S(1)}) all-reduce(f32[1024]{0:T(1024)S(1)} %exponential_multiply_fusion, f32[1024]{0:T(1024)S(1)} %get-tuple-element.150), channel_id=1, replica_groups=mesh['seq'=8,'head'=16] {'seq','head'}, use_global_device_ids=true, to_apply=%region_11.12 | all-reduce | flops 2048 | bytes 16384 | tf_op jit(solution)/shard_map/psum | solution.py:120
  (44 shorter events, 5.9 us)
Async XLA Ops:
  6.5 46.7 %copy-start = (bf16[256,6144]{1,0:T(8,128)(2,1)S(1)}, bf16[256,6144]{1,0:T(8,128)(2,1)}, u32[]{:S(2)}) copy-start(bf16[256,6144]{1,0:T(8,128)(2,1)} %param.18) | copy-start | bytes 9437188
  6.5 35.2 %all-gather.9.cloned.1.call-start = ((), (), s32[]{:S(2)}) async-start(), calls=%async_computation.1 | async-start | bytes 1179648 | tf_op jit(solution)/shard_map/all_gather | solution.py:9
  14.7 323.4 %all-gather.11.cloned.1.call-start = ((), (), s32[]{:S(2)}) async-start(), calls=%async_computation.2 | async-start | bytes 53477376 | tf_op jit(solution)/shard_map/all_gather | solution.py:93
  55.5 0.7 copy-start.2
  55.5 376.1 %all-gather.7.cloned.1.call-start = ((), (), s32[]{:S(2)}) async-start(), calls=%async_computation | async-start | bytes 12681216 | tf_op jit(solution)/shard_map/all_gather | solution.py:111
  338.1 20.0 %copy-start.3 = (s32[1024]{0:T(1024)S(1)}, s32[1024]{0:T(1024)}, u32[]{:S(2)}) copy-start(s32[1024]{0:T(1024)} %param.21) | copy-start | bytes 12292
  431.6 152.1 %copy-start.1 = (bf16[256,6144]{1,0:T(8,128)(2,1)S(1)}, bf16[256,6144]{1,0:T(8,128)(2,1)}, u32[]{:S(2)}) copy-start(bf16[256,6144]{1,0:T(8,128)(2,1)} %param.18) | copy-start | bytes 9437188
Sparse Core Ops, SparseCore 0:
  14.8 26.9 all-gather.8
  55.6 282.4 all-gather.10
  358.2 73.3 all-gather.6
